TPU v7x, 32 devices: a whole 2x2x4 slice. The times are simulated.
32 devices in a mesh: groups: 2 (over x), tile: 16 (over z, y, core).
Axes of the slice: x: 2, y: 2, z: 4, core: 2. Of those that a mesh axis runs over, the one named last changes fastest.
Arguments:
- source: bfloat16 [512, 2, 69, 128], P('tile', 'groups'), parts along dimension 1, may hold values from -42 to 42
- weights: bfloat16 [1536, 128, 128], P('tile'), may hold values from -0.5 to 0.5
- block_source: int32 [1536], P('tile'), may hold values from 0 to 31
- block_target: int32 [1536], P('tile'), may hold values from 0 to 511, as said below
- edge_flip: int32 [16, 2], P('tile'), may hold values 0 or 1
- norm_gain: float32 [69], replicated, may hold values from 0.1 to 1.9
- first_kernel: bfloat16 [9, 69, 69], replicated, may hold values from -0.25 to 0.25
- second_kernel: bfloat16 [9, 69, 69], replicated, may hold values from -0.25 to 0.25
Outputs:
- gridded: bfloat16 [512, 2, 69, 128], P('tile', 'groups'), parts along dimension 1
- smoothed: bfloat16 [512, 2, 69, 128], P('tile', 'groups'), parts along dimension 1
There are 2 independent parts, one for each index of `groups`. A program takes and returns all parts, laid end to end along the dimension named above; an argument that names none is the same for every part. Nothing has to cross between parts.
Inputs may be any that keep to these rules, and one draw needn't show every extreme that they name: `block_target`: band d lies at the latitude of tile position p = d mod 2, in column d // 2. Its entries name exactly 64 distinct target rows, all in tiles c * 2 + p or c * 2 + p + 1 (any column c, positions below 2). One band names at most 8 distinct rows of one tile, and every band at position 1 names exactly 8 rows of each tile at its own position.
All inputs are finite; a program needn't handle non-finite values. No bound on the sum of `edge_flip` on one device may be relied on, other than what follows from the above.
Results may differ from a plain program's by a relative error of at most 0.001.
The roundings to bfloat16 on the way count: a program that leaves them out, or rounds other values in their place, can miss the bound.
Values may be sent and summed in bfloat16 or wider, within the bound.
No kernel may reach another device: no remote copies, remote signals or barrier semaphores. Data moves between devices by JAX's collectives and lax.ppermute only.
A program may use at most 64 MiB of HBM per device.

v0:
```python
import functools

import jax
import jax.numpy as jnp
from jax import lax
from jax.experimental import pallas as pl
from jax.experimental.pallas import tpu as pltpu
from jax.sharding import PartitionSpec as P

BLOCK = 128
CHANNELS = 69
PADDED = 72
WIDE = 80
ROWS = 32
TILE_COLS = 8
CAP = 8
GROUPS = 2 * TILE_COLS
SLOTS = GROUPS * CAP
CHUNK = 32
MARK = CHANNELS
EPSILON = 1e-05
VMEM_LIMIT = 40 * 1024 * 1024
FULL_VMEM = 60 * 1024 * 1024


def vmem():
    return pl.BlockSpec(memory_space=pltpu.VMEM)


def smem():
    return pl.BlockSpec(memory_space=pltpu.SMEM)


def split(value, size):
    if size & (size - 1) == 0:
        return value >> (size.bit_length() - 1), value & (size - 1)
    return lax.div(value, size), lax.rem(value, size)


def lanes(shape):
    return lax.broadcasted_iota(jnp.int32, shape, len(shape) - 1)


def regrid_kernel(column_rows, target_ref, index_ref, source_hbm, weight_hbm, *rest):
    same_out, next_outs = rest[0], rest[1 : 1 + TILE_COLS]
    (
        source,
        weight,
        wide,
        field,
        sums,
        rounded,
        slot_of,
        used,
        entry_slot,
        entry_fresh,
        source_sem,
        weight_sems,
        out_sems,
    ) = rest[1 + TILE_COLS :]
    entries = weight.shape[0]
    chunks = entries // CHUNK
    tile = lax.axis_index("tile")
    column, position = split(tile, column_rows)

    source_copy = pltpu.make_async_copy(source_hbm, source, source_sem)
    source_copy.start()

    def chunk_copy(chunk):
        part = pl.ds(chunk * CHUNK, CHUNK)
        return pltpu.make_async_copy(weight_hbm.at[part], weight.at[part], weight_sems.at[chunk])

    for chunk in range(chunks):
        chunk_copy(chunk).start()

    for key in range(GROUPS * ROWS):
        slot_of[key] = -1
    for group in range(GROUPS):
        used[group] = 0

    def plan(entry, carry):
        target = target_ref[entry]
        owner, row = split(target, ROWS)
        owner_column, owner_position = split(owner, column_rows)
        same = owner_position == position
        group = jnp.where(same, owner_column, TILE_COLS + (owner_column ^ column))
        key = group * ROWS + row
        known = slot_of[key]
        count = used[group]
        fresh = known < 0
        slot = jnp.where(fresh, group * CAP + count, known)
        slot_of[key] = slot
        used[group] = jnp.where(fresh, count + 1, count)
        entry_slot[entry] = slot
        entry_fresh[entry] = fresh.astype(jnp.int32)
        return carry

    lax.fori_loop(0, entries, plan, 0, unroll=4)

    tail = PADDED - 8
    for slot in range(SLOTS):
        rounded[slot, tail:] = jnp.full((8, BLOCK), ROWS, jnp.bfloat16)
    wide[pl.ds(CHANNELS * ROWS, (PADDED - CHANNELS) * ROWS), :] = jnp.zeros(
        ((PADDED - CHANNELS) * ROWS, BLOCK), jnp.float32
    )
    nothing = jnp.zeros((WIDE - PADDED, BLOCK), jnp.float32)
    source_copy.wait()
    wide[pl.ds(0, CHANNELS * ROWS), :] = source[...].astype(jnp.float32)
    for row in range(ROWS):
        block = wide[pl.ds(row, PADDED, stride=ROWS), :]
        field[row] = jnp.concatenate([block, nothing], axis=0).astype(jnp.bfloat16)
    is_mark = lax.broadcasted_iota(jnp.int32, (8, BLOCK), 0) == MARK - tail

    for chunk in range(chunks):
        chunk_copy(chunk).wait()
        for entry in range(chunk * CHUNK, (chunk + 1) * CHUNK):
            slot = entry_slot[entry]
            row = split(target_ref[entry], ROWS)[1]
            product = jnp.dot(
                field[index_ref[entry]], weight[entry], preferred_element_type=jnp.float32
            )
            total = jnp.where(entry_fresh[entry] == 1, 0.0, sums[slot]) + product[:PADDED]
            sums[slot] = total
            marked = jnp.where(is_mark, row.astype(jnp.float32), total[tail:])
            rounded[slot] = jnp.concatenate([total[:tail], marked], axis=0).astype(jnp.bfloat16)
    copies = [
        pltpu.make_async_copy(
            rounded.at[pl.ds(0, SLOTS // 2)], same_out, out_sems.at[0]
        )
    ]
    for group in range(TILE_COLS):
        part = rounded.at[pl.ds((TILE_COLS + group) * CAP, CAP)]
        copies.append(pltpu.make_async_copy(part, next_outs[group], out_sems.at[1 + group]))
    for copy in copies:
        copy.start()
    for copy in copies:
        copy.wait()


def regrid(target, source_index, field, weights, column_rows):
    piece = jax.ShapeDtypeStruct((CAP, PADDED, BLOCK), jnp.bfloat16)
    same = jax.ShapeDtypeStruct((TILE_COLS * CAP, PADDED, BLOCK), jnp.bfloat16)
    hbm = pl.BlockSpec(memory_space=pl.ANY)
    entries = weights.shape[0]
    return pl.pallas_call(
        functools.partial(regrid_kernel, column_rows),
        in_specs=[smem(), smem(), hbm, hbm],
        out_specs=[hbm] * (1 + TILE_COLS),
        out_shape=[same] + [piece] * TILE_COLS,
        scratch_shapes=[
            pltpu.VMEM(field.shape, jnp.bfloat16),
            pltpu.VMEM(weights.shape, jnp.bfloat16),
            pltpu.VMEM((PADDED * ROWS, BLOCK), jnp.float32),
            pltpu.VMEM((ROWS, WIDE, BLOCK), jnp.bfloat16),
            pltpu.VMEM((SLOTS, PADDED, BLOCK), jnp.float32),
            pltpu.VMEM((SLOTS, PADDED, BLOCK), jnp.bfloat16),
            pltpu.SMEM((GROUPS * ROWS,), jnp.int32),
            pltpu.SMEM((GROUPS,), jnp.int32),
            pltpu.SMEM((entries,), jnp.int32),
            pltpu.SMEM((entries,), jnp.int32),
            pltpu.SemaphoreType.DMA,
            pltpu.SemaphoreType.DMA((entries // CHUNK,)),
            pltpu.SemaphoreType.DMA((1 + TILE_COLS,)),
        ],
        compiler_params=pltpu.CompilerParams(vmem_limit_bytes=FULL_VMEM),
        name="regrid",
    )(target, source_index, field, weights)


def gather_kernel(column_rows, flip_ref, gain_ref, same, *rest):
    nexts = rest[:TILE_COLS]
    (
        gridded,
        normed,
        upward,
        downward,
        strip_out,
        summed,
        marks,
        rows,
        mark_sem,
    ) = rest[TILE_COLS:]
    position = lax.rem(lax.axis_index("tile"), column_rows)
    half = SLOTS // 2
    lane = lanes((1, BLOCK))
    mark = jnp.zeros((1, BLOCK), jnp.float32)
    for slot in range(SLOTS):
        piece = same.at[slot] if slot < half else nexts[slot // CAP - TILE_COLS].at[slot % CAP]
        mark = jnp.where(lane == slot, piece[MARK : MARK + 1].astype(jnp.float32), mark)
    marks[...] = mark.astype(jnp.int32)
    copy = pltpu.make_async_copy(marks, rows, mark_sem)
    copy.start()
    summed[...] = jnp.zeros_like(summed)
    copy.wait()

    def add(slot, piece):
        row = rows[0, slot]
        summed[row] = summed[row] + piece.astype(jnp.float32)

    def add_same(step, carry):
        for at in range(CAP):
            add(step * CAP + at, same[step * CAP + at])
        return carry

    lax.fori_loop(0, TILE_COLS, add_same, 0)

    @pl.when(position > 0)
    def _():
        for group in range(TILE_COLS):
            for place in range(CAP):
                add(half + group * CAP + place, nexts[group][place])

    gain = gain_ref[...]
    channel = lax.broadcasted_iota(jnp.int32, (PADDED, BLOCK), 0)
    nothing = jnp.zeros((WIDE - PADDED, BLOCK), jnp.float32)
    lane = lanes((WIDE, BLOCK))
    strip = jnp.zeros((WIDE, BLOCK), jnp.bfloat16)
    for row in range(ROWS):
        rounded = summed[row].astype(jnp.bfloat16)
        gridded[row] = rounded
        value = rounded.astype(jnp.float32)
        value = jnp.where(channel < CHANNELS, value, 0.0)
        square = jnp.sum(value * value, axis=0, keepdims=True) * (1.0 / CHANNELS)
        scaled = value * lax.rsqrt(square + EPSILON) * gain
        scaled = jnp.concatenate([scaled, nothing], axis=0).astype(jnp.bfloat16)
        normed[row] = scaled
        if row < 2:
            upward[row] = scaled
        if row >= ROWS - 2:
            downward[row - ROWS + 2] = scaled
        for place, column in enumerate(STRIP_COLUMNS):
            at = place * ROWS + row
            strip = jnp.where(lane == at, pltpu.roll(scaled, (at - column) % BLOCK, 1), strip)
    strip = strip.astype(jnp.float32)
    channel = lax.broadcasted_iota(jnp.int32, (WIDE, BLOCK), 0)
    for side in range(2):
        strip = jnp.where(channel == CHANNELS + side, flip_ref[0, side].astype(jnp.float32), strip)
    strip = strip.astype(jnp.bfloat16)
    upward[2] = strip
    downward[2] = strip
    strip_out[...] = strip


GRIDDED = jax.ShapeDtypeStruct((ROWS, PADDED, BLOCK), jnp.bfloat16)
FIELD = jax.ShapeDtypeStruct((ROWS, WIDE, BLOCK), jnp.bfloat16)
RIM = jax.ShapeDtypeStruct((3, WIDE, BLOCK), jnp.bfloat16)
STRIP_COLUMNS = (0, 1, BLOCK - 2, BLOCK - 1)
STRIP = jax.ShapeDtypeStruct((WIDE, BLOCK), jnp.bfloat16)


def gather_rows(column_rows, edge_flip, gain, same, nexts):
    return pl.pallas_call(
        functools.partial(gather_kernel, column_rows),
        in_specs=[smem()] + [vmem()] * (2 + TILE_COLS),
        out_specs=[vmem()] * 5,
        out_shape=[GRIDDED, FIELD, RIM, RIM, STRIP],
        scratch_shapes=[
            pltpu.VMEM((ROWS + 1, PADDED, BLOCK), jnp.float32),
            pltpu.VMEM((1, SLOTS), jnp.int32),
            pltpu.SMEM((1, SLOTS), jnp.int32),
            pltpu.SemaphoreType.DMA,
        ],
        compiler_params=pltpu.CompilerParams(vmem_limit_bytes=VMEM_LIMIT),
        name="gather_rows",
    )(edge_flip, gain, same, *nexts)


def turn_kernel(field, out, turned):
    for row in range(ROWS):
        turned[pl.ds(row, PADDED, stride=ROWS), :] = field[row].astype(jnp.float32)
    out[...] = turned[pl.ds(0, CHANNELS * ROWS), :].astype(jnp.bfloat16)


def channels_first(field):
    return pl.pallas_call(
        turn_kernel,
        in_specs=[vmem()],
        out_specs=vmem(),
        out_shape=jax.ShapeDtypeStruct((CHANNELS * ROWS, BLOCK), jnp.bfloat16),
        scratch_shapes=[pltpu.VMEM((PADDED * ROWS, BLOCK), jnp.float32)],
        compiler_params=pltpu.CompilerParams(vmem_limit_bytes=VMEM_LIMIT),
        name="channels_first",
    )(field)


def shifted_columns(value, left_end, right_end):
    lane = lanes((WIDE, BLOCK))
    left = jnp.where(lane == 0, left_end, pltpu.roll(value, 1, 1))
    right = jnp.where(lane == BLOCK - 1, right_end, pltpu.roll(value, BLOCK - 1, 1))
    return jnp.concatenate([left, value, right], axis=0)


def tap_sums(taps, one, two):
    both = jnp.concatenate([one, two], axis=1)
    result = jnp.dot(taps, both, preferred_element_type=jnp.float32)
    return result[:, :BLOCK], result[:, BLOCK:]


def row_tap(sums, at):
    return sums[at * WIDE : (at + 1) * WIDE]


def activated(value):
    return jax.nn.gelu(value).astype(jnp.bfloat16)


def inner_kernel(taps_ref, field, hidden, ends, sides, partial):
    taps = taps_ref[...]
    blank = jnp.zeros((WIDE, BLOCK), jnp.bfloat16)
    for row in range(0, ROWS, 2):
        partial[row], partial[row + 1] = tap_sums(
            taps,
            shifted_columns(field[row], blank, blank),
            shifted_columns(field[row + 1], blank, blank),
        )
    lane = lanes((WIDE, BLOCK))
    west = jnp.zeros((WIDE, BLOCK), jnp.float32)
    east = jnp.zeros((WIDE, BLOCK), jnp.float32)
    for row in range(ROWS):
        value = partial[row, WIDE : 2 * WIDE]
        if row > 0:
            value = value + partial[row - 1, :WIDE]
        if row < ROWS - 1:
            value = value + partial[row + 1, 2 * WIDE :]
        if row == 0:
            ends[0] = value
        elif row == ROWS - 1:
            ends[1] = value
        else:
            hidden[row] = activated(value)
        west = jnp.where(lane == row, pltpu.roll(value, row, 1), west)
        east = jnp.where(lane == row, pltpu.roll(value, row + 1, 1), east)
    hidden[0] = blank
    hidden[ROWS - 1] = blank
    sides[0] = west
    sides[1] = east


def inner_convolution(taps, field):
    pair = jax.ShapeDtypeStruct((2, WIDE, BLOCK), jnp.float32)
    return pl.pallas_call(
        inner_kernel,
        in_specs=[vmem()] * 2,
        out_specs=[vmem()] * 3,
        out_shape=[FIELD, pair, pair],
        scratch_shapes=[pltpu.VMEM((ROWS, 3 * WIDE, BLOCK), jnp.float32)],
        compiler_params=pltpu.CompilerParams(vmem_limit_bytes=VMEM_LIMIT),
        cost_estimate=pl.CostEstimate(
            flops=2 * 9 * WIDE * WIDE * ROWS * BLOCK, bytes_accessed=2 << 20, transcendentals=0
        ),
        name="inner_convolution",
    )(taps, field)


def strip_plan(column_rows):
    if column_rows == 2:
        return [], 3, 1
    return [-2, 2], column_rows, 2


def conv_kernel(
    column_rows,
    first_taps_ref,
    second_taps_ref,
    field,
    gridded,
    inner,
    ends_ref,
    sides_ref,
    above,
    below,
    own_strip,
    *rest,
):
    near, far, reach = strip_plan(column_rows)
    near_strips, (west_pack, east_pack) = rest[: len(near)], rest[len(near) : len(near) + 2]
    smoothed, hidden, partial, turned = rest[len(near) + 2 :]
    count = lax.axis_size("tile")
    tile = lax.axis_index("tile")
    lane = lanes((WIDE, BLOCK))
    last = ROWS + 1
    R = column_rows
    blank = jnp.zeros((WIDE, BLOCK), jnp.bfloat16)

    strips = {-1: above[2], 0: own_strip[...], 1: below[2]}
    strips.update((shift, ref[...]) for shift, ref in zip(near, near_strips))
    for at in range(-reach, reach + 1):
        strips[at - far], strips[at + far] = west_pack[at + reach], east_pack[at + reach]

    def place(shift):
        return lax.rem(tile + shift + count, count)

    def ends(shift, before, after, middle):
        before = jnp.where(place(shift) > 0, before, blank)
        after = jnp.where(place(shift) < count - 1, after, blank)
        return jnp.where(lane == 0, before, jnp.where(lane == last, after, middle))

    memo = {}

    def padded_column(shift, which):
        if (shift, which) not in memo:
            base = which * ROWS
            memo[shift, which] = ends(
                shift,
                pltpu.roll(strips[shift - 1], (1 - base - ROWS) % BLOCK, 1),
                pltpu.roll(strips[shift + 1], (last - base) % BLOCK, 1),
                pltpu.roll(strips[shift], (1 - base) % BLOCK, 1),
            )
        return memo[shift, which]

    row_id = lax.broadcasted_iota(jnp.int32, (BLOCK, BLOCK), 0)
    reversal = (row_id + lanes((BLOCK, BLOCK)) == last).astype(jnp.bfloat16)

    def reversed_lanes(planes):
        stacked = jnp.concatenate(planes, axis=0)
        turned_round = jnp.dot(stacked, reversal, preferred_element_type=jnp.float32)
        return [row_tap(turned_round, at) for at in range(len(planes))]

    def choose(shift, which, turned_round, plain):
        flips = strips[shift].astype(jnp.float32)[CHANNELS + which : CHANNELS + which + 1]
        return jnp.where(flips > 0.5, turned_round, plain.astype(jnp.float32)).astype(jnp.bfloat16)

    west_of = {shift: (shift - R, 3) for shift in {-1, 0, 1, R - 1, R, R + 1}}
    east_of = {shift: (shift + R, 0) for shift in {-1, 0, 1, -R - 1, -R, -R + 1}}
    keys = sorted(set(west_of.values()) | set(east_of.values()))
    flipped = dict(zip(keys, reversed_lanes([padded_column(*key) for key in keys])))
    west = {
        shift: choose(shift, 0, flipped[west_of[shift]], padded_column(*west_of[shift]))
        for shift in sorted(west_of)
    }
    east = {
        shift: choose(shift, 1, flipped[east_of[shift]], padded_column(*east_of[shift]))
        for shift in sorted(east_of)
    }

    def columns(value, west_plane, west_row, east_plane, east_row):
        return shifted_columns(
            value,
            pltpu.roll(west_plane, (BLOCK - west_row) % BLOCK, 1),
            pltpu.roll(east_plane, BLOCK - 1 - east_row, 1),
        )

    def along(result):
        return (
            row_tap(result, 0)
            + pltpu.roll(row_tap(result, 1), BLOCK - 1, 1)
            + pltpu.roll(row_tap(result, 2), BLOCK - 2, 1)
        )

    first_taps = first_taps_ref[...]
    up = [jnp.where(tile > 0, above[at], blank) for at in range(2)]
    down = [jnp.where(tile < count - 1, below[at], blank) for at in range(2)]
    from_up, from_down = tap_sums(
        first_taps, shifted_columns(up[1], blank, blank), shifted_columns(down[0], blank, blank)
    )
    from_up, from_down = row_tap(from_up, 0), row_tap(from_down, 2)
    from_west, from_east = tap_sums(
        first_taps,
        jnp.concatenate([west[0], blank, blank], axis=0),
        jnp.concatenate([blank, blank, east[0]], axis=0),
    )
    from_west, from_east = along(from_west), along(from_east)
    first = ends_ref[0] + from_up
    first = first + jnp.where(lane == 0, from_west, 0.0)
    first = first + jnp.where(lane == BLOCK - 1, pltpu.roll(from_east, BLOCK - 1, 1), 0.0)
    final = ends_ref[1] + from_down
    final = final + jnp.where(lane == 0, pltpu.roll(from_west, BLOCK - ROWS + 1, 1), 0.0)
    final = final + jnp.where(lane == BLOCK - 1, pltpu.roll(from_east, BLOCK - ROWS, 1), 0.0)
    hidden[1] = activated(first)
    hidden[ROWS] = activated(final)
    first_column = activated(sides_ref[0] + from_west)
    last_column = activated(sides_ref[1] + from_east)
    for row in range(1, ROWS - 1):
        value = jnp.where(lane == 0, pltpu.roll(first_column, BLOCK - row, 1), inner[row])
        hidden[row + 1] = jnp.where(
            lane == BLOCK - 1, pltpu.roll(last_column, BLOCK - 1 - row, 1), value
        )

    upper = jnp.zeros((WIDE, BLOCK), jnp.float32)
    lower = jnp.zeros((WIDE, BLOCK), jnp.float32)
    for at, (high, low) in enumerate(
        [(up[0], field[ROWS - 1]), (up[1], down[0]), (field[0], down[1])]
    ):
        from_row = ROWS - 1 + at
        one, two = tap_sums(
            first_taps,
            columns(high, west[-1], from_row, east[-1], from_row),
            columns(low, west[1], at, east[1], at),
        )
        upper += row_tap(one, at)
        lower += row_tap(two, at)
    hidden[0] = jnp.where(tile > 0, activated(upper), blank)
    hidden[last] = jnp.where(tile < count - 1, activated(lower), blank)

    west_hidden, east_hidden = {}, {}
    for at in (-1, 0, 1):
        q = at - R
        one = jnp.concatenate([padded_column(q, 2), padded_column(q, 3), east[q]], axis=0)
        q = at + R
        two = jnp.concatenate([west[q], padded_column(q, 0), padded_column(q, 1)], axis=0)
        one, two = tap_sums(first_taps, one, two)
        west_hidden[at], east_hidden[at] = activated(along(one)), activated(along(two))

    def hidden_side(shift, values):
        return ends(
            shift,
            pltpu.roll(values[-1], BLOCK - ROWS + 1, 1),
            pltpu.roll(values[1], last, 1),
            pltpu.roll(values[0], 1, 1),
        )

    plain = [hidden_side(-R, west_hidden), hidden_side(R, east_hidden)]
    west_side, east_side = [
        choose(0, which, turned_side, plain[which])
        for which, turned_side in enumerate(reversed_lanes(plain))
    ]

    second_taps = second_taps_ref[...]
    for p in range(0, ROWS + 2, 2):
        partial[p], partial[p + 1] = tap_sums(
            second_taps,
            columns(hidden[p], west_side, p, east_side, p),
            columns(hidden[p + 1], west_side, p + 1, east_side, p + 1),
        )
    for row in range(ROWS):
        branch = (
            partial[row, :PADDED]
            + partial[row + 1, WIDE : WIDE + PADDED]
            + partial[row + 2, 2 * WIDE : 2 * WIDE + PADDED]
        )
        turned[pl.ds(row, PADDED, stride=ROWS), :] = gridded[row].astype(jnp.float32) + branch
    smoothed[...] = turned[pl.ds(0, CHANNELS * ROWS), :].astype(jnp.bfloat16)


def convolutions(column_rows, *operands):
    return pl.pallas_call(
        functools.partial(conv_kernel, column_rows),
        in_specs=[vmem()] * len(operands),
        out_specs=vmem(),
        out_shape=jax.ShapeDtypeStruct((CHANNELS * ROWS, BLOCK), jnp.bfloat16),
        scratch_shapes=[
            pltpu.VMEM((ROWS + 2, WIDE, BLOCK), jnp.bfloat16),
            pltpu.VMEM((ROWS + 2, 3 * WIDE, BLOCK), jnp.float32),
            pltpu.VMEM((PADDED * ROWS, BLOCK), jnp.float32),
        ],
        compiler_params=pltpu.CompilerParams(vmem_limit_bytes=VMEM_LIMIT),
        name="convolutions",
    )(*operands)


def tap_matrix(kernel):
    pad = WIDE - CHANNELS
    taps = jnp.pad(kernel, ((0, 0), (0, pad), (0, pad))).reshape(3, 3, WIDE, WIDE)
    return taps.transpose(0, 2, 1, 3).reshape(3 * WIDE, 3 * WIDE)


def from_shift(value, shift):
    count = lax.axis_size("tile")
    return lax.ppermute(value, "tile", [(i, (i - shift) % count) for i in range(count)])


def per_device(
    source, weights, block_source, block_target, edge_flip, norm_gain, first_kernel, second_kernel
):
    count = lax.axis_size("tile")
    column_rows = count // TILE_COLS
    field = source.reshape(ROWS, CHANNELS, BLOCK).transpose(1, 0, 2).reshape(-1, BLOCK)
    same, *nexts = regrid(block_target, block_source, field, weights, column_rows)

    for across in reversed(range(TILE_COLS)):
        pairs = [
            (c * column_rows + p, (c ^ across) * column_rows + p + 1)
            for c in range(TILE_COLS)
            for p in range(column_rows - 1)
        ]
        nexts[across] = lax.ppermute(nexts[across], "tile", pairs)
    same = lax.all_to_all(
        same,
        "tile",
        0,
        0,
        axis_index_groups=[
            [c * column_rows + p for c in range(TILE_COLS)] for p in range(column_rows)
        ],
        tiled=True,
    )

    gain = jnp.broadcast_to(
        jnp.pad(norm_gain, (0, PADDED - CHANNELS))[:, None], (PADDED, BLOCK)
    )
    first_taps, second_taps = tap_matrix(first_kernel), tap_matrix(second_kernel)
    same, nexts, gain, first_taps, second_taps = lax.optimization_barrier(
        (same, nexts, gain, first_taps, second_taps)
    )
    gridded, normed, upward, downward, strip = gather_rows(
        column_rows, edge_flip, gain, same, nexts
    )
    rims = [from_shift(downward, -1), from_shift(upward, 1)]
    near, far, reach = strip_plan(column_rows)
    strips = [from_shift(strip, shift) for shift in near]
    inner = inner_convolution(first_taps, normed)
    held = {-1: rims[0][2], 0: strip, 1: rims[1][2], **dict(zip(near, strips))}
    pack = jnp.stack([held[at] for at in range(-reach, reach + 1)])
    pack, inner = lax.optimization_barrier((pack, inner))
    strips += [from_shift(pack, -far), from_shift(pack, far)]
    gridded_out = channels_first(gridded)
    smoothed = convolutions(
        column_rows, first_taps, second_taps, normed, gridded, *inner, *rims, strip, *strips
    )

    def placed(value):
        return value.reshape(CHANNELS, ROWS, BLOCK).transpose(1, 0, 2)[:, None]

    return placed(gridded_out), placed(smoothed)


def solution(mesh):
    in_specs = (
        P("tile", "groups", None, None),
        P("tile", None, None),
        P("tile"),
        P("tile"),
        P("tile", None),
        P(),
        P(),
        P(),
    )
    out_specs = (P("tile", "groups", None, None), P("tile", "groups", None, None))
    return jax.shard_map(
        per_device, mesh=mesh, in_specs=in_specs, out_specs=out_specs, check_vma=False
    )
```

profile of v0, /device:TPU:1, one launch (start us, length us, event | category | flops | bytes accessed | tf_op | source)
XLA Modules:
  0.0 71.4 jit_solution(1490728918279802733)
XLA Ops:
  0.6 6.2 %regrid.1 = (bf16[64,72,128]{2,1,0:T(8,128)(2,1)}, bf16[8,72,128]{2,1,0:T(8,128)(2,1)}, bf16[8,72,128]{2,1,0:T(8,128)(2,1)}, bf16[8,72,128]{2,1,0:T(8,128)(2,1)}...) custom-call(s32[96]{0:T(128)} %target_ref.1, ...), custom_call_target="tpu_custom_call" | custom-call | tf_op jit(solution)/shard_map/regrid/pallas_call | solution.py:145
  6.8 0.0 copy-start.8
  6.8 0.0 copy-start.7
  6.8 0.0 copy-start.6
  6.8 0.0 copy-start.5
  6.8 0.0 copy-start.4
  6.8 0.0 copy-start.3
  6.9 0.0 copy-start.1
  6.9 0.0 copy-start.2
  6.9 6.5 %all-to-all-start = ((bf16[64,72,128]{2,1,0:T(8,128)(2,1)}), bf16[64,72,128]{2,1,0:T(8,128)(2,1)S(1)}, u32[]{:S(2)}, u32[]{:S(2)}) async-start(bf16[64,72,128]{2,1,0:T(8,128)(2,1)} %get-tuple-element.35), calls=%async_computation | async-start | bytes 2359296 | tf_op jit(solution)/shard_map/all_to_all | solution.py:577
  13.4 0.0 copy-start
  13.4 1.3 %collective-permute-start = (bf16[8,72,128]{2,1,0:T(8,128)(2,1)S(1)}, bf16[8,72,128]{2,1,0:T(8,128)(2,1)S(1)}, u32[]{:S(2)}, u32[]{:S(2)}) collective-permute-start(bf16[8,72,128]{2,1,0:T(8,128)(2,1)S(1)} %copy-done.8), channel_id=1, source_target_pairs={{0,1},{2,3},{4,5},{6,7},{8,9},{10,11},{12,13},{14,15},{16,17},{18,... | collective-permute-start | bytes 442376 | tf_op jit(solution)/shard_map/ppermute | solution.py:576
  14.7 0.0 copy-done.7
  14.7 1.3 %collective-permute-start.1 = (bf16[8,72,128]{2,1,0:T(8,128)(2,1)S(1)}, bf16[8,72,128]{2,1,0:T(8,128)(2,1)S(1)}, u32[]{:S(2)}, u32[]{:S(2)}) collective-permute-start(bf16[8,72,128]{2,1,0:T(8,128)(2,1)S(1)} %copy-done.7), channel_id=1, source_target_pairs={{0,3},{2,1},{4,7},{6,5},{8,11},{10,9},{12,15},{14,13},{16,19},{18,... | collective-permute-start | bytes 442376 | tf_op jit(solution)/shard_map/ppermute | solution.py:576
  16.0 0.0 copy-done.6
  16.1 1.3 %collective-permute-start.2 = (bf16[8,72,128]{2,1,0:T(8,128)(2,1)S(1)}, bf16[8,72,128]{2,1,0:T(8,128)(2,1)S(1)}, u32[]{:S(2)}, u32[]{:S(2)}) collective-permute-start(bf16[8,72,128]{2,1,0:T(8,128)(2,1)S(1)} %copy-done.6), channel_id=1, source_target_pairs={{0,5},{2,7},{4,1},{6,3},{8,13},{10,15},{12,9},{14,11},{16,21},{18,... | collective-permute-start | bytes 442376 | tf_op jit(solution)/shard_map/ppermute | solution.py:576
  17.4 1.3 %collective-permute-start.3 = (bf16[8,72,128]{2,1,0:T(8,128)(2,1)}, bf16[8,72,128]{2,1,0:T(8,128)(2,1)S(1)}, u32[]{:S(2)}, u32[]{:S(2)}) collective-permute-start(bf16[8,72,128]{2,1,0:T(8,128)(2,1)} %get-tuple-element.39), channel_id=1, source_target_pairs={{0,7},{2,5},{4,3},{6,1},{8,15},{10,13},{12,11},{14,9},{16,23},{18,... | collective-permute-start | bytes 442376 | tf_op jit(solution)/shard_map/ppermute | solution.py:576
  18.7 1.3 %collective-permute-start.4 = (bf16[8,72,128]{2,1,0:T(8,128)(2,1)}, bf16[8,72,128]{2,1,0:T(8,128)(2,1)S(1)}, u32[]{:S(2)}, u32[]{:S(2)}) collective-permute-start(bf16[8,72,128]{2,1,0:T(8,128)(2,1)} %get-tuple-element.40), channel_id=1, source_target_pairs={{0,9},{2,11},{4,13},{6,15},{8,1},{10,3},{12,5},{14,7},{16,25},{18,... | collective-permute-start | bytes 442376 | tf_op jit(solution)/shard_map/ppermute | solution.py:576
  20.0 0.0 collective-permute-done.rest_0_
  20.0 1.3 %collective-permute-start.5 = (bf16[8,72,128]{2,1,0:T(8,128)(2,1)S(1)}, bf16[8,72,128]{2,1,0:T(8,128)(2,1)S(1)}, u32[]{:S(2)}, u32[]{:S(2)}) collective-permute-start(bf16[8,72,128]{2,1,0:T(8,128)(2,1)S(1)} %copy-done.5), channel_id=1, source_target_pairs={{0,11},{2,9},{4,15},{6,13},{8,3},{10,1},{12,7},{14,5},{16,27},{18,... | collective-permute-start | bytes 442376 | tf_op jit(solution)/shard_map/ppermute | solution.py:576
  21.3 4.0 %collective-permute-done.1.rest_1_ = bf16[8,72,128]{2,1,0:T(8,128)(2,1)S(1)} collective-permute-done((bf16[8,72,128]{2,1,0:T(8,128)(2,1)S(1)}, bf16[8,72,128]{2,1,0:T(8,128)(2,1)S(1)}, u32[]{:S(2)}, u32[]{:S(2)}) %collective-permute-start.1) | collective-permute-done | bytes 147488 | tf_op jit(solution)/shard_map/ppermute | solution.py:576
  25.3 0.0 copy-done.4
  25.3 1.3 %collective-permute-start.6 = (bf16[8,72,128]{2,1,0:T(8,128)(2,1)S(1)}, bf16[8,72,128]{2,1,0:T(8,128)(2,1)S(1)}, u32[]{:S(2)}, u32[]{:S(2)}) collective-permute-start(bf16[8,72,128]{2,1,0:T(8,128)(2,1)S(1)} %copy-done.4), channel_id=1, source_target_pairs={{0,13},{2,15},{4,9},{6,11},{8,5},{10,7},{12,1},{14,3},{16,29},{18,... | collective-permute-start | bytes 442376 | tf_op jit(solution)/shard_map/ppermute | solution.py:576
  26.6 4.7 %collective-permute-done.2.rest_2_ = bf16[8,72,128]{2,1,0:T(8,128)(2,1)S(1)} collective-permute-done((bf16[8,72,128]{2,1,0:T(8,128)(2,1)S(1)}, bf16[8,72,128]{2,1,0:T(8,128)(2,1)S(1)}, u32[]{:S(2)}, u32[]{:S(2)}) %collective-permute-start.2) | collective-permute-done | bytes 147488 | tf_op jit(solution)/shard_map/ppermute | solution.py:576
  31.3 1.3 %collective-permute-start.7 = (bf16[8,72,128]{2,1,0:T(8,128)(2,1)S(1)}, bf16[8,72,128]{2,1,0:T(8,128)(2,1)S(1)}, u32[]{:S(2)}, u32[]{:S(2)}) collective-permute-start(bf16[8,72,128]{2,1,0:T(8,128)(2,1)S(1)} %copy-done.3), channel_id=1, source_target_pairs={{0,15},{2,13},{4,11},{6,9},{8,7},{10,5},{12,3},{14,1},{16,31},{18,... | collective-permute-start | bytes 442376 | tf_op jit(solution)/shard_map/ppermute | solution.py:576
  32.6 0.1 copy.17
  32.7 0.2 reshape.32.taps_ref.first_taps_ref
  32.9 0.1 copy.16
  33.0 0.2 reshape.34.second_taps_ref
  33.2 2.8 %collective-permute-done.3.rest_3_ = bf16[8,72,128]{2,1,0:T(8,128)(2,1)S(1)} collective-permute-done((bf16[8,72,128]{2,1,0:T(8,128)(2,1)}, bf16[8,72,128]{2,1,0:T(8,128)(2,1)S(1)}, u32[]{:S(2)}, u32[]{:S(2)}) %collective-permute-start.3) | collective-permute-done | bytes 147488 | tf_op jit(solution)/shard_map/ppermute | solution.py:576
  36.1 14.1 %collective-permute-done.4.rest_4_ = bf16[8,72,128]{2,1,0:T(8,128)(2,1)S(1)} collective-permute-done((bf16[8,72,128]{2,1,0:T(8,128)(2,1)}, bf16[8,72,128]{2,1,0:T(8,128)(2,1)S(1)}, u32[]{:S(2)}, u32[]{:S(2)}) %collective-permute-start.4) | collective-permute-done | bytes 147488 | tf_op jit(solution)/shard_map/ppermute | solution.py:576
  50.1 2.5 %collective-permute-done.5.rest_5_ = bf16[8,72,128]{2,1,0:T(8,128)(2,1)S(1)} collective-permute-done((bf16[8,72,128]{2,1,0:T(8,128)(2,1)S(1)}, bf16[8,72,128]{2,1,0:T(8,128)(2,1)S(1)}, u32[]{:S(2)}, u32[]{:S(2)}) %collective-permute-start.5) | collective-permute-done | bytes 147488 | tf_op jit(solution)/shard_map/ppermute | solution.py:576
  52.7 0.0 collective-permute-done.6.rest_6_
  52.7 0.0 collective-permute-done.7.rest_7_
  52.7 0.0 all-to-all-done.same
  52.7 0.1 broadcast_in_dim.12.gain_ref
  52.8 2.8 %gather_rows.1 = (bf16[32,72,128]{2,1,0:T(8,128)(2,1)S(1)}, bf16[32,80,128]{2,1,0:T(8,128)(2,1)S(1)}, bf16[3,80,128]{2,1,0:T(8,128)(2,1)S(1)}, bf16[3,80,128]{2,1,0:T(8,128)(2,1)S(1)}, bf16[80,128]{1,0:T(8,128)(2,1)S(1)}) custom-call(s32[1,2]{1,0:T(1,128)S(1)} %copy-done, f32[72,128]{1,0:T(8,128)S(1)} %broadcast_in_dim.12.gain_ref, ...), custom_call_target="tpu_custom_call" | custom-call | tf_op jit(solution)/shard_map/gather_rows/pallas_call | solution.py:252
  55.5 0.1 collective-permute-start.8
  55.6 0.5 collective-permute-start.9
  56.1 1.2 %inner_convolution.1 = (bf16[32,80,128]{2,1,0:T(8,128)(2,1)S(1)}, f32[2,80,128]{2,1,0:T(8,128)S(1)}, f32[2,80,128]{2,1,0:T(8,128)S(1)}) custom-call(bf16[240,240]{1,0:T(8,128)(2,1)S(1)} %reshape.32.taps_ref.first_taps_ref, bf16[32,80,128]{2,1,0:T(8,128)(2,1)S(1)} %get-tuple-element.57.field), custom_call_target="tpu_custom_call" | custom-call | flops 471859200 | bytes 2097152 | tf_op jit(solution)/shard_map/inner_convolution/pallas_call | solution.py:341
  57.3 0.0 collective-permute-done.8.above
  57.3 2.0 %collective-permute-done.9.below = bf16[3,80,128]{2,1,0:T(8,128)(2,1)S(1)} collective-permute-done((bf16[3,80,128]{2,1,0:T(8,128)(2,1)S(1)}, bf16[3,80,128]{2,1,0:T(8,128)(2,1)S(1)}, u32[]{:S(2)}, u32[]{:S(2)}) %collective-permute-start.9) | collective-permute-done | bytes 61472 | tf_op jit(solution)/shard_map/ppermute | solution.py:559
  59.3 0.9 %collective-permute-start.11 = (bf16[3,80,128]{2,1,0:T(8,128)(2,1)S(1)}, bf16[3,80,128]{2,1,0:T(8,128)(2,1)S(1)}, u32[]{:S(2)}, u32[]{:S(2)}) collective-permute-start(bf16[3,80,128]{2,1,0:T(8,128)(2,1)S(1)} %pad_maximum_fusion), channel_id=1, source_target_pairs={{0,13},{1,14},{2,15},{3,0},{4,1},{5,2},{6,3},{7,4},{8,5},{9,6},{10... | collective-permute-start | bytes 184328 | tf_op jit(solution)/shard_map/ppermute | solution.py:559
  60.2 1.2 %collective-permute-start.10 = (bf16[3,80,128]{2,1,0:T(8,128)(2,1)S(1)}, bf16[3,80,128]{2,1,0:T(8,128)(2,1)S(1)}, u32[]{:S(2)}, u32[]{:S(2)}) collective-permute-start(bf16[3,80,128]{2,1,0:T(8,128)(2,1)S(1)} %pad_maximum_fusion), channel_id=1, source_target_pairs={{0,3},{1,4},{2,5},{3,6},{4,7},{5,8},{6,9},{7,10},{8,11},{9,12},{10... | collective-permute-start | bytes 184328 | tf_op jit(solution)/shard_map/ppermute | solution.py:559
  61.4 2.0 %channels_first.1 = bf16[2208,128]{1,0:T(8,128)(2,1)} custom-call(bf16[32,72,128]{2,1,0:T(8,128)(2,1)S(1)} %get-tuple-element.54.field.gridded), custom_call_target="tpu_custom_call" | custom-call | tf_op jit(solution)/shard_map/channels_first/pallas_call | solution.py:275
  63.4 0.0 collective-permute-done.11.rest_1_
  63.4 4.3 %collective-permute-done.10.rest_0_ = bf16[3,80,128]{2,1,0:T(8,128)(2,1)S(1)} collective-permute-done((bf16[3,80,128]{2,1,0:T(8,128)(2,1)S(1)}, bf16[3,80,128]{2,1,0:T(8,128)(2,1)S(1)}, u32[]{:S(2)}, u32[]{:S(2)}) %collective-permute-start.10) | collective-permute-done | bytes 61472 | tf_op jit(solution)/shard_map/ppermute | solution.py:559
  67.7 3.7 %convolutions.1 = bf16[2208,128]{1,0:T(8,128)(2,1)} custom-call(bf16[240,240]{1,0:T(8,128)(2,1)S(1)} %reshape.32.taps_ref.first_taps_ref, bf16[240,240]{1,0:T(8,128)(2,1)S(1)} %reshape.34.second_taps_ref, bf16[32,80,128]{2,1,0:T(8,128)(2,1)S(1)} %get-tuple-element.57.field, bf16[32,72,128]{2,1,0:T(8,128)(2,1)S(1)} %get-tuple-element.54.field.gridded, ...), custom_call_target="tpu_custom_call" | custom-call | tf_op jit(solution)/shard_map/convolutions/pallas_call | solution.py:536
  (14 shorter events, 0.1 us)
Async XLA Ops:
  6.8 6.6 %copy-start.8 = (bf16[8,72,128]{2,1,0:T(8,128)(2,1)S(1)}, bf16[8,72,128]{2,1,0:T(8,128)(2,1)}, u32[]{:S(2)}) copy-start(bf16[8,72,128]{2,1,0:T(8,128)(2,1)} %get-tuple-element.36) | copy-start | bytes 442372
  6.8 7.9 %copy-start.7 = (bf16[8,72,128]{2,1,0:T(8,128)(2,1)S(1)}, bf16[8,72,128]{2,1,0:T(8,128)(2,1)}, u32[]{:S(2)}) copy-start(bf16[8,72,128]{2,1,0:T(8,128)(2,1)} %get-tuple-element.37) | copy-start | bytes 442372
  6.8 9.2 %copy-start.6 = (bf16[8,72,128]{2,1,0:T(8,128)(2,1)S(1)}, bf16[8,72,128]{2,1,0:T(8,128)(2,1)}, u32[]{:S(2)}) copy-start(bf16[8,72,128]{2,1,0:T(8,128)(2,1)} %get-tuple-element.38) | copy-start | bytes 442372
  6.8 13.1 %copy-start.5 = (bf16[8,72,128]{2,1,0:T(8,128)(2,1)S(1)}, bf16[8,72,128]{2,1,0:T(8,128)(2,1)}, u32[]{:S(2)}) copy-start(bf16[8,72,128]{2,1,0:T(8,128)(2,1)} %get-tuple-element.41) | copy-start | bytes 442372
  6.8 18.5 %copy-start.4 = (bf16[8,72,128]{2,1,0:T(8,128)(2,1)S(1)}, bf16[8,72,128]{2,1,0:T(8,128)(2,1)}, u32[]{:S(2)}) copy-start(bf16[8,72,128]{2,1,0:T(8,128)(2,1)} %get-tuple-element.42) | copy-start | bytes 442372
  6.8 24.4 %copy-start.3 = (bf16[8,72,128]{2,1,0:T(8,128)(2,1)S(1)}, bf16[8,72,128]{2,1,0:T(8,128)(2,1)}, u32[]{:S(2)}) copy-start(bf16[8,72,128]{2,1,0:T(8,128)(2,1)} %get-tuple-element.43) | copy-start | bytes 442372
  6.9 25.7 %copy-start.1 = (bf16[9,69,69]{2,1,0:T(8,128)(2,1)S(1)}, bf16[9,69,69]{2,1,0:T(8,128)(2,1)}, u32[]{:S(2)}) copy-start(bf16[9,69,69]{2,1,0:T(8,128)(2,1)} %param.14) | copy-start | bytes 257098
  6.9 26.0 %copy-start.2 = (bf16[9,69,69]{2,1,0:T(8,128)(2,1)S(1)}, bf16[9,69,69]{2,1,0:T(8,128)(2,1)}, u32[]{:S(2)}) copy-start(bf16[9,69,69]{2,1,0:T(8,128)(2,1)} %param.15) | copy-start | bytes 257098
  6.9 45.8 %all-to-all-start = ((bf16[64,72,128]{2,1,0:T(8,128)(2,1)}), bf16[64,72,128]{2,1,0:T(8,128)(2,1)S(1)}, u32[]{:S(2)}, u32[]{:S(2)}) async-start(bf16[64,72,128]{2,1,0:T(8,128)(2,1)} %get-tuple-element.35), calls=%async_computation | async-start | bytes 2359296 | tf_op jit(solution)/shard_map/all_to_all | solution.py:577
  13.4 19.8 %copy-start.9 = (f32[69]{0:T(128)S(1)}, f32[69]{0:T(128)}, u32[]{:S(2)}) copy-start(f32[69]{0:T(128)} %param.13) | copy-start | bytes 832
  13.4 39.3 %copy-start = (s32[1,2]{1,0:T(1,128)S(1)}, s32[1,2]{1,0:T(1,128)}, u32[]{:S(2)}) copy-start(s32[1,2]{1,0:T(1,128)} %flip_ref.1) | copy-start | bytes 28
  13.4 6.5 %collective-permute-start = (bf16[8,72,128]{2,1,0:T(8,128)(2,1)S(1)}, bf16[8,72,128]{2,1,0:T(8,128)(2,1)S(1)}, u32[]{:S(2)}, u32[]{:S(2)}) collective-permute-start(bf16[8,72,128]{2,1,0:T(8,128)(2,1)S(1)} %copy-done.8), channel_id=1, source_target_pairs={{0,1},{2,3},{4,5},{6,7},{8,9},{10,11},{12,13},{14,15},{16,17},{18,... | collective-permute-start | bytes 442376 | tf_op jit(solution)/shard_map/ppermute | solution.py:576
  14.7 10.6 %collective-permute-start.1 = (bf16[8,72,128]{2,1,0:T(8,128)(2,1)S(1)}, bf16[8,72,128]{2,1,0:T(8,128)(2,1)S(1)}, u32[]{:S(2)}, u32[]{:S(2)}) collective-permute-start(bf16[8,72,128]{2,1,0:T(8,128)(2,1)S(1)} %copy-done.7), channel_id=1, source_target_pairs={{0,3},{2,1},{4,7},{6,5},{8,11},{10,9},{12,15},{14,13},{16,19},{18,... | collective-permute-start | bytes 442376 | tf_op jit(solution)/shard_map/ppermute | solution.py:576
  16.1 15.2 %collective-permute-start.2 = (bf16[8,72,128]{2,1,0:T(8,128)(2,1)S(1)}, bf16[8,72,128]{2,1,0:T(8,128)(2,1)S(1)}, u32[]{:S(2)}, u32[]{:S(2)}) collective-permute-start(bf16[8,72,128]{2,1,0:T(8,128)(2,1)S(1)} %copy-done.6), channel_id=1, source_target_pairs={{0,5},{2,7},{4,1},{6,3},{8,13},{10,15},{12,9},{14,11},{16,21},{18,... | collective-permute-start | bytes 442376 | tf_op jit(solution)/shard_map/ppermute | solution.py:576
  17.4 18.7 %collective-permute-start.3 = (bf16[8,72,128]{2,1,0:T(8,128)(2,1)}, bf16[8,72,128]{2,1,0:T(8,128)(2,1)S(1)}, u32[]{:S(2)}, u32[]{:S(2)}) collective-permute-start(bf16[8,72,128]{2,1,0:T(8,128)(2,1)} %get-tuple-element.39), channel_id=1, source_target_pairs={{0,7},{2,5},{4,3},{6,1},{8,15},{10,13},{12,11},{14,9},{16,23},{18,... | collective-permute-start | bytes 442376 | tf_op jit(solution)/shard_map/ppermute | solution.py:576
  18.7 31.5 %collective-permute-start.4 = (bf16[8,72,128]{2,1,0:T(8,128)(2,1)}, bf16[8,72,128]{2,1,0:T(8,128)(2,1)S(1)}, u32[]{:S(2)}, u32[]{:S(2)}) collective-permute-start(bf16[8,72,128]{2,1,0:T(8,128)(2,1)} %get-tuple-element.40), channel_id=1, source_target_pairs={{0,9},{2,11},{4,13},{6,15},{8,1},{10,3},{12,5},{14,7},{16,25},{18,... | collective-permute-start | bytes 442376 | tf_op jit(solution)/shard_map/ppermute | solution.py:576
  20.0 32.7 %collective-permute-start.5 = (bf16[8,72,128]{2,1,0:T(8,128)(2,1)S(1)}, bf16[8,72,128]{2,1,0:T(8,128)(2,1)S(1)}, u32[]{:S(2)}, u32[]{:S(2)}) collective-permute-start(bf16[8,72,128]{2,1,0:T(8,128)(2,1)S(1)} %copy-done.5), channel_id=1, source_target_pairs={{0,11},{2,9},{4,15},{6,13},{8,3},{10,1},{12,7},{14,5},{16,27},{18,... | collective-permute-start | bytes 442376 | tf_op jit(solution)/shard_map/ppermute | solution.py:576
  25.3 27.4 %collective-permute-start.6 = (bf16[8,72,128]{2,1,0:T(8,128)(2,1)S(1)}, bf16[8,72,128]{2,1,0:T(8,128)(2,1)S(1)}, u32[]{:S(2)}, u32[]{:S(2)}) collective-permute-start(bf16[8,72,128]{2,1,0:T(8,128)(2,1)S(1)} %copy-done.4), channel_id=1, source_target_pairs={{0,13},{2,15},{4,9},{6,11},{8,5},{10,7},{12,1},{14,3},{16,29},{18,... | collective-permute-start | bytes 442376 | tf_op jit(solution)/shard_map/ppermute | solution.py:576
  31.3 21.4 %collective-permute-start.7 = (bf16[8,72,128]{2,1,0:T(8,128)(2,1)S(1)}, bf16[8,72,128]{2,1,0:T(8,128)(2,1)S(1)}, u32[]{:S(2)}, u32[]{:S(2)}) collective-permute-start(bf16[8,72,128]{2,1,0:T(8,128)(2,1)S(1)} %copy-done.3), channel_id=1, source_target_pairs={{0,15},{2,13},{4,11},{6,9},{8,7},{10,5},{12,3},{14,1},{16,31},{18,... | collective-permute-start | bytes 442376 | tf_op jit(solution)/shard_map/ppermute | solution.py:576
  55.5 1.8 %collective-permute-start.8 = (bf16[3,80,128]{2,1,0:T(8,128)(2,1)S(1)}, bf16[3,80,128]{2,1,0:T(8,128)(2,1)S(1)}, u32[]{:S(2)}, u32[]{:S(2)}) collective-permute-start(bf16[3,80,128]{2,1,0:T(8,128)(2,1)S(1)} %get-tuple-element.58), channel_id=1, source_target_pairs={{0,1},{1,2},{2,3},{3,4},{4,5},{5,6},{6,7},{7,8},{8,9},{9,10},{10,1... | collective-permute-start | bytes 184328 | tf_op jit(solution)/shard_map/ppermute | solution.py:559
  55.6 3.7 %collective-permute-start.9 = (bf16[3,80,128]{2,1,0:T(8,128)(2,1)S(1)}, bf16[3,80,128]{2,1,0:T(8,128)(2,1)S(1)}, u32[]{:S(2)}, u32[]{:S(2)}) collective-permute-start(bf16[3,80,128]{2,1,0:T(8,128)(2,1)S(1)} %get-tuple-element.60), channel_id=1, source_target_pairs={{0,15},{1,0},{2,1},{3,2},{4,3},{5,4},{6,5},{7,6},{8,7},{9,8},{10,9... | collective-permute-start | bytes 184328 | tf_op jit(solution)/shard_map/ppermute | solution.py:559
  59.3 4.1 %collective-permute-start.11 = (bf16[3,80,128]{2,1,0:T(8,128)(2,1)S(1)}, bf16[3,80,128]{2,1,0:T(8,128)(2,1)S(1)}, u32[]{:S(2)}, u32[]{:S(2)}) collective-permute-start(bf16[3,80,128]{2,1,0:T(8,128)(2,1)S(1)} %pad_maximum_fusion), channel_id=1, source_target_pairs={{0,13},{1,14},{2,15},{3,0},{4,1},{5,2},{6,3},{7,4},{8,5},{9,6},{10... | collective-permute-start | bytes 184328 | tf_op jit(solution)/shard_map/ppermute | solution.py:559
  60.2 7.5 %collective-permute-start.10 = (bf16[3,80,128]{2,1,0:T(8,128)(2,1)S(1)}, bf16[3,80,128]{2,1,0:T(8,128)(2,1)S(1)}, u32[]{:S(2)}, u32[]{:S(2)}) collective-permute-start(bf16[3,80,128]{2,1,0:T(8,128)(2,1)S(1)} %pad_maximum_fusion), channel_id=1, source_target_pairs={{0,3},{1,4},{2,5},{3,6},{4,7},{5,8},{6,9},{7,10},{8,11},{9,12},{10... | collective-permute-start | bytes 184328 | tf_op jit(solution)/shard_map/ppermute | solution.py:559
where the time goes:
time: 71.7 us; the launch traced here: 71.4 us
  waiting for transfers between devices  34.4 us (48%)
  starting transfers between devices  19.5 us (27%)
  Pallas kernels  15.8 us (22%)
  between operations  0.95 us (1%)
    ppermute x8, waiting for transfers between devices, per_device(): nexts[across] = lax.ppermute(nexts[across], 'tile', pairs)  28.2 us
    ppermute x8, starting transfers between devices, per_device(): nexts[across] = lax.ppermute(nexts[across], 'tile', pairs)  10.3 us
    all_to_all x1, starting transfers between devices, per_device(): lax.all_to_all(same, 'tile', 0, 0, axis_index_groups=[[c * column_rows +...  6.53 us
    ppermute x4, waiting for transfers between devices, from_shift(): lax.ppermute(value, 'tile', [(i, (i - shift) % count) for i in range(coun...  6.26 us
    pallas_call x1, Pallas kernels, regrid(): pl.pallas_call(functools.partial(regrid_kernel, column_rows), in_specs=[s...  6.16 us
    pallas_call x1, Pallas kernels, convolutions(): pl.pallas_call(functools.partial(conv_kernel, column_rows), in_specs=[vme...  3.72 us
    pallas_call x1, Pallas kernels, gather_rows(): pl.pallas_call(functools.partial(gather_kernel, column_rows), in_specs=[s...  2.75 us
    ppermute x4, starting transfers between devices, from_shift(): lax.ppermute(value, 'tile', [(i, (i - shift) % count) for i in range(coun...  2.66 us
  transfers between devices with their start and end apart: 13, of which 7 were waited for; matrix products, arithmetic and copies ran while one was open for 1% of the time, Pallas kernels for 4%

commit v1 on v0

--- a/solution.py
+++ b/solution.py
@@ -12,12 +12,14 @@
 PADDED = 72
 WIDE = 80
 ROWS = 32
+ROW_BITS = 5
 TILE_COLS = 8
 CAP = 8
 GROUPS = 2 * TILE_COLS
 SLOTS = GROUPS * CAP
 CHUNK = 32
 MARK = CHANNELS
+EARLY = 6
 EPSILON = 1e-05
 VMEM_LIMIT = 40 * 1024 * 1024
 FULL_VMEM = 60 * 1024 * 1024
@@ -41,7 +43,9 @@
     return lax.broadcasted_iota(jnp.int32, shape, len(shape) - 1)
 
 
-def regrid_kernel(column_rows, target_ref, index_ref, source_hbm, weight_hbm, *rest):
+def regrid_kernel(
+    column_rows, target_ref, index_ref, target_row_ref, source_hbm, weight_hbm, *rest
+):
     same_out, next_outs = rest[0], rest[1 : 1 + TILE_COLS]
     (
         source,
@@ -50,10 +54,9 @@
         field,
         sums,
         rounded,
-        slot_of,
-        used,
-        entry_slot,
-        entry_fresh,
+        plan,
+        plan_scalars,
+        plan_sem,
         source_sem,
         weight_sems,
         out_sems,
@@ -73,29 +76,30 @@
     for chunk in range(chunks):
         chunk_copy(chunk).start()
 
-    for key in range(GROUPS * ROWS):
-        slot_of[key] = -1
-    for group in range(GROUPS):
-        used[group] = 0
-
-    def plan(entry, carry):
-        target = target_ref[entry]
-        owner, row = split(target, ROWS)
-        owner_column, owner_position = split(owner, column_rows)
-        same = owner_position == position
-        group = jnp.where(same, owner_column, TILE_COLS + (owner_column ^ column))
-        key = group * ROWS + row
-        known = slot_of[key]
-        count = used[group]
-        fresh = known < 0
-        slot = jnp.where(fresh, group * CAP + count, known)
-        slot_of[key] = slot
-        used[group] = jnp.where(fresh, count + 1, count)
-        entry_slot[entry] = slot
-        entry_fresh[entry] = fresh.astype(jnp.int32)
-        return carry
-
-    lax.fori_loop(0, entries, plan, 0, unroll=4)
+    target = target_row_ref[...]
+    owner, row = split(target, ROWS)
+    owner_column, owner_position = split(owner, column_rows)
+    group = jnp.where(
+        owner_position == position, owner_column, TILE_COLS + (owner_column ^ column)
+    )
+    key = group * ROWS + row
+    square = (entries, entries)
+    down = lax.broadcasted_iota(jnp.int32, square, 0)
+    along = lanes(square)
+    key_along = jnp.broadcast_to(key.astype(jnp.float32), square)
+    key_down = jnp.broadcast_to(
+        jnp.sum(jnp.where(down == along, key_along, 0.0), axis=1, keepdims=True), square
+    )
+    equal = key_along == key_down
+    doubles = jnp.sum(jnp.where(equal & (along < down), 1.0, 0.0), axis=1, keepdims=True)
+    in_group = (key_down.astype(jnp.int32) >> ROW_BITS) == (key_along.astype(jnp.int32) >> ROW_BITS)
+    below = in_group & (key_down < key_along) & (jnp.broadcast_to(doubles, square) == 0.0)
+    rank = jnp.sum(jnp.where(below, 1.0, 0.0), axis=0, keepdims=True)
+    mentions = jnp.sum(jnp.where(equal & (down < along), 1.0, 0.0), axis=0, keepdims=True)
+    slots = group * CAP + rank.astype(jnp.int32)
+    plan[...] = slots + jnp.where(mentions == 0.0, SLOTS, 0)
+    plan_copy = pltpu.make_async_copy(plan, plan_scalars, plan_sem)
+    plan_copy.start()
 
     tail = PADDED - 8
     for slot in range(SLOTS):
@@ -110,16 +114,18 @@
         block = wide[pl.ds(row, PADDED, stride=ROWS), :]
         field[row] = jnp.concatenate([block, nothing], axis=0).astype(jnp.bfloat16)
     is_mark = lax.broadcasted_iota(jnp.int32, (8, BLOCK), 0) == MARK - tail
+    plan_copy.wait()
 
     for chunk in range(chunks):
         chunk_copy(chunk).wait()
         for entry in range(chunk * CHUNK, (chunk + 1) * CHUNK):
-            slot = entry_slot[entry]
+            code = plan_scalars[0, entry]
+            slot = code & (SLOTS - 1)
             row = split(target_ref[entry], ROWS)[1]
             product = jnp.dot(
                 field[index_ref[entry]], weight[entry], preferred_element_type=jnp.float32
             )
-            total = jnp.where(entry_fresh[entry] == 1, 0.0, sums[slot]) + product[:PADDED]
+            total = jnp.where(code >= SLOTS, 0.0, sums[slot]) + product[:PADDED]
             sums[slot] = total
             marked = jnp.where(is_mark, row.astype(jnp.float32), total[tail:])
             rounded[slot] = jnp.concatenate([total[:tail], marked], axis=0).astype(jnp.bfloat16)
@@ -144,7 +150,7 @@
     entries = weights.shape[0]
     return pl.pallas_call(
         functools.partial(regrid_kernel, column_rows),
-        in_specs=[smem(), smem(), hbm, hbm],
+        in_specs=[smem(), smem(), vmem(), hbm, hbm],
         out_specs=[hbm] * (1 + TILE_COLS),
         out_shape=[same] + [piece] * TILE_COLS,
         scratch_shapes=[
@@ -154,61 +160,88 @@
             pltpu.VMEM((ROWS, WIDE, BLOCK), jnp.bfloat16),
             pltpu.VMEM((SLOTS, PADDED, BLOCK), jnp.float32),
             pltpu.VMEM((SLOTS, PADDED, BLOCK), jnp.bfloat16),
-            pltpu.SMEM((GROUPS * ROWS,), jnp.int32),
-            pltpu.SMEM((GROUPS,), jnp.int32),
-            pltpu.SMEM((entries,), jnp.int32),
-            pltpu.SMEM((entries,), jnp.int32),
+            pltpu.VMEM((1, entries), jnp.int32),
+            pltpu.SMEM((1, entries), jnp.int32),
+            pltpu.SemaphoreType.DMA,
             pltpu.SemaphoreType.DMA,
             pltpu.SemaphoreType.DMA((entries // CHUNK,)),
             pltpu.SemaphoreType.DMA((1 + TILE_COLS,)),
         ],
         compiler_params=pltpu.CompilerParams(vmem_limit_bytes=FULL_VMEM),
         name="regrid",
-    )(target, source_index, field, weights)
-
-
-def gather_kernel(column_rows, flip_ref, gain_ref, same, *rest):
-    nexts = rest[:TILE_COLS]
+    )(target, source_index, target.reshape(1, -1), field, weights)
+
+
+def scatter_rows(summed, marks, rows, sem, pieces):
+    lane = lanes((1, BLOCK))
+    mark = jnp.zeros((1, BLOCK), jnp.float32)
+    for at, piece in enumerate(pieces):
+        mark = jnp.where(lane == at, piece[MARK : MARK + 1].astype(jnp.float32), mark)
+    marks[...] = mark.astype(jnp.int32)
+    copy = pltpu.make_async_copy(marks, rows, sem)
+    copy.start()
+    copy.wait()
+    for at, piece in enumerate(pieces):
+        row = rows[0, at]
+        summed[row] = summed[row] + piece[...].astype(jnp.float32)
+
+
+def scatter_scratch():
+    return [
+        pltpu.VMEM((1, SLOTS), jnp.int32),
+        pltpu.SMEM((1, SLOTS), jnp.int32),
+        pltpu.SemaphoreType.DMA,
+    ]
+
+
+SUMMED = (ROWS + 1, PADDED, BLOCK)
+
+
+def early_kernel(column_rows, same, *rest):
+    nexts, (summed, marks, rows, sem) = rest[:EARLY], rest[EARLY:]
+    position = lax.rem(lax.axis_index("tile"), column_rows)
+    summed[...] = jnp.zeros_like(summed)
+    scatter_rows(summed, marks, rows, sem, [same.at[slot] for slot in range(SLOTS // 2)])
+
+    @pl.when(position > 0)
+    def _():
+        pieces = [piece.at[place] for piece in nexts for place in range(CAP)]
+        scatter_rows(summed, marks, rows, sem, pieces)
+
+
+def early_rows(column_rows, same, nexts):
+    return pl.pallas_call(
+        functools.partial(early_kernel, column_rows),
+        in_specs=[vmem()] * (1 + EARLY),
+        out_specs=vmem(),
+        out_shape=jax.ShapeDtypeStruct(SUMMED, jnp.float32),
+        scratch_shapes=scatter_scratch(),
+        compiler_params=pltpu.CompilerParams(vmem_limit_bytes=VMEM_LIMIT),
+        cost_estimate=pl.CostEstimate(flops=SLOTS << 14, bytes_accessed=4 << 20, transcendentals=0),
+        name="early_rows",
+    )(same, *nexts)
+
+
+def gather_kernel(column_rows, flip_ref, gain_ref, before, *rest):
+    nexts = rest[: TILE_COLS - EARLY]
     (
         gridded,
         normed,
         upward,
         downward,
         strip_out,
-        summed,
+        late,
         marks,
         rows,
-        mark_sem,
-    ) = rest[TILE_COLS:]
+        sem,
+    ) = rest[TILE_COLS - EARLY :]
     position = lax.rem(lax.axis_index("tile"), column_rows)
-    half = SLOTS // 2
-    lane = lanes((1, BLOCK))
-    mark = jnp.zeros((1, BLOCK), jnp.float32)
-    for slot in range(SLOTS):
-        piece = same.at[slot] if slot < half else nexts[slot // CAP - TILE_COLS].at[slot % CAP]
-        mark = jnp.where(lane == slot, piece[MARK : MARK + 1].astype(jnp.float32), mark)
-    marks[...] = mark.astype(jnp.int32)
-    copy = pltpu.make_async_copy(marks, rows, mark_sem)
-    copy.start()
-    summed[...] = jnp.zeros_like(summed)
-    copy.wait()
-
-    def add(slot, piece):
-        row = rows[0, slot]
-        summed[row] = summed[row] + piece.astype(jnp.float32)
-
-    def add_same(step, carry):
-        for at in range(CAP):
-            add(step * CAP + at, same[step * CAP + at])
-        return carry
-
-    lax.fori_loop(0, TILE_COLS, add_same, 0)
+    late[...] = jnp.zeros_like(late)
 
     @pl.when(position > 0)
     def _():
-        for group in range(TILE_COLS):
-            for place in range(CAP):
-                add(half + group * CAP + place, nexts[group][place])
+        pieces = [piece.at[place] for piece in nexts for place in range(CAP)]
+        scatter_rows(late, marks, rows, sem, pieces)
 
     gain = gain_ref[...]
     channel = lax.broadcasted_iota(jnp.int32, (PADDED, BLOCK), 0)
@@ -216,7 +249,7 @@
     lane = lanes((WIDE, BLOCK))
     strip = jnp.zeros((WIDE, BLOCK), jnp.bfloat16)
     for row in range(ROWS):
-        rounded = summed[row].astype(jnp.bfloat16)
+        rounded = (before[row] + late[row]).astype(jnp.bfloat16)
         gridded[row] = rounded
         value = rounded.astype(jnp.float32)
         value = jnp.where(channel < CHANNELS, value, 0.0)
@@ -248,21 +281,16 @@
 STRIP = jax.ShapeDtypeStruct((WIDE, BLOCK), jnp.bfloat16)
 
 
-def gather_rows(column_rows, edge_flip, gain, same, nexts):
+def gather_rows(column_rows, edge_flip, gain, before, nexts):
     return pl.pallas_call(
         functools.partial(gather_kernel, column_rows),
-        in_specs=[smem()] + [vmem()] * (2 + TILE_COLS),
+        in_specs=[smem()] + [vmem()] * (2 + len(nexts)),
         out_specs=[vmem()] * 5,
         out_shape=[GRIDDED, FIELD, RIM, RIM, STRIP],
-        scratch_shapes=[
-            pltpu.VMEM((ROWS + 1, PADDED, BLOCK), jnp.float32),
-            pltpu.VMEM((1, SLOTS), jnp.int32),
-            pltpu.SMEM((1, SLOTS), jnp.int32),
-            pltpu.SemaphoreType.DMA,
-        ],
+        scratch_shapes=[pltpu.VMEM(SUMMED, jnp.float32), *scatter_scratch()],
         compiler_params=pltpu.CompilerParams(vmem_limit_bytes=VMEM_LIMIT),
         name="gather_rows",
-    )(edge_flip, gain, same, *nexts)
+    )(edge_flip, gain, before, *nexts)
 
 
 def turn_kernel(field, out, turned):
@@ -567,7 +595,7 @@
     field = source.reshape(ROWS, CHANNELS, BLOCK).transpose(1, 0, 2).reshape(-1, BLOCK)
     same, *nexts = regrid(block_target, block_source, field, weights, column_rows)
 
-    for across in reversed(range(TILE_COLS)):
+    for across in range(TILE_COLS):
         pairs = [
             (c * column_rows + p, (c ^ across) * column_rows + p + 1)
             for c in range(TILE_COLS)
@@ -589,11 +617,12 @@
         jnp.pad(norm_gain, (0, PADDED - CHANNELS))[:, None], (PADDED, BLOCK)
     )
     first_taps, second_taps = tap_matrix(first_kernel), tap_matrix(second_kernel)
-    same, nexts, gain, first_taps, second_taps = lax.optimization_barrier(
-        (same, nexts, gain, first_taps, second_taps)
+    before = early_rows(column_rows, same, nexts[:EARLY])
+    nexts, gain, first_taps, second_taps = lax.optimization_barrier(
+        (nexts[EARLY:], gain, first_taps, second_taps)
     )
     gridded, normed, upward, downward, strip = gather_rows(
-        column_rows, edge_flip, gain, same, nexts
+        column_rows, edge_flip, gain, before, nexts
     )
     rims = [from_shift(downward, -1), from_shift(upward, 1)]
     near, far, reach = strip_plan(column_rows)

time: 71.7 us -> 74.2 us (1.035)
  starting transfers between devices: 19.5 us -> 22.3 us
  waiting for transfers between devices: 34.4 us -> 32.3 us
  Pallas kernels: 15.8 us -> 17.1 us
    ppermute x4, waiting for transfers between devices: 6.26 us -> 3.47 us  [from_shift(): lax.ppermute(value, 'tile', [(i, (i - shift) % count) for i in range(coun...]
    ppermute x4, starting transfers between devices: 2.66 us -> 5.41 us  [from_shift(): lax.ppermute(value, 'tile', [(i, (i - shift) % count) for i in range(coun...]
    pallas_call x0 -> x1, Pallas kernels: none -> 1.93 us  [early_rows(): pl.pallas_call(functools.partial(early_kernel, column_rows), in_specs=[vm...]
  transfers between devices with their start and end apart: 13 -> 13, of which waited for: 7 -> 8; matrix products, arithmetic and copies ran while one was open for 1% -> 1% of each run, Pallas kernels for 4% -> 4%
where the time goes in v1:
time: 74.2 us; the launch traced here: 73.4 us
  waiting for transfers between devices  32.3 us (44%)
  starting transfers between devices  22.3 us (30%)
  Pallas kernels  17.1 us (23%)
  between operations  0.95 us (1%)
    ppermute x8, waiting for transfers between devices, per_device(): nexts[across] = lax.ppermute(nexts[across], 'tile', pairs)  28.8 us
    ppermute x8, starting transfers between devices, per_device(): nexts[across] = lax.ppermute(nexts[across], 'tile', pairs)  10.3 us
    all_to_all x1, starting transfers between devices, per_device(): lax.all_to_all(same, 'tile', 0, 0, axis_index_groups=[[c * column_rows +...  6.53 us
    pallas_call x1, Pallas kernels, regrid(): pl.pallas_call(functools.partial(regrid_kernel, column_rows), in_specs=[s...  6.21 us
    ppermute x4, starting transfers between devices, from_shift(): lax.ppermute(value, 'tile', [(i, (i - shift) % count) for i in range(coun...  5.41 us
    pallas_call x1, Pallas kernels, convolutions(): pl.pallas_call(functools.partial(conv_kernel, column_rows), in_specs=[vme...  3.73 us
    ppermute x4, waiting for transfers between devices, from_shift(): lax.ppermute(value, 'tile', [(i, (i - shift) % count) for i in range(coun...  3.47 us
    pallas_call x1, Pallas kernels, gather_rows(): pl.pallas_call(functools.partial(gather_kernel, column_rows), in_specs=[s...  2.11 us
  transfers between devices with their start and end apart: 13, of which 8 were waited for; matrix products, arithmetic and copies ran while one was open for 1% of the time, Pallas kernels for 4%

profile of v1, /device:TPU:1, one launch (start us, length us, event | category | flops | bytes accessed | tf_op | source)
XLA Modules:
  0.0 73.4 jit_solution(10280827383144840851)
XLA Ops:
  0.6 6.2 %regrid.1 = (bf16[64,72,128]{2,1,0:T(8,128)(2,1)}, bf16[8,72,128]{2,1,0:T(8,128)(2,1)}, bf16[8,72,128]{2,1,0:T(8,128)(2,1)}, bf16[8,72,128]{2,1,0:T(8,128)(2,1)}...) custom-call(s32[96]{0:T(128)} %target_ref.1, ...), custom_call_target="tpu_custom_call" | custom-call | tf_op jit(solution)/shard_map/regrid/pallas_call | solution.py:151
  6.8 0.0 copy-start.8
  6.9 0.0 copy-start.7
  6.9 0.0 copy-start.6
  6.9 0.0 copy-start.5
  6.9 0.0 copy-start.4
  6.9 0.0 copy-start.3
  6.9 0.0 copy-start.1
  6.9 0.0 copy-start.2
  6.9 6.5 %all-to-all-start = ((bf16[64,72,128]{2,1,0:T(8,128)(2,1)}), bf16[64,72,128]{2,1,0:T(8,128)(2,1)S(1)}, u32[]{:S(2)}, u32[]{:S(2)}) async-start(bf16[64,72,128]{2,1,0:T(8,128)(2,1)} %get-tuple-element.31), calls=%async_computation | async-start | bytes 2359296 | tf_op jit(solution)/shard_map/all_to_all | solution.py:605
  13.5 1.3 %collective-permute-start.2 = (bf16[8,72,128]{2,1,0:T(8,128)(2,1)S(1)}, bf16[8,72,128]{2,1,0:T(8,128)(2,1)S(1)}, u32[]{:S(2)}, u32[]{:S(2)}) collective-permute-start(bf16[8,72,128]{2,1,0:T(8,128)(2,1)S(1)} %copy-done.8), channel_id=1, source_target_pairs={{0,1},{2,3},{4,5},{6,7},{8,9},{10,11},{12,13},{14,15},{16,17},{18,... | collective-permute-start | bytes 442376 | tf_op jit(solution)/shard_map/ppermute | solution.py:604
  14.8 1.3 %collective-permute-start = (bf16[8,72,128]{2,1,0:T(8,128)(2,1)S(1)}, bf16[8,72,128]{2,1,0:T(8,128)(2,1)S(1)}, u32[]{:S(2)}, u32[]{:S(2)}) collective-permute-start(bf16[8,72,128]{2,1,0:T(8,128)(2,1)S(1)} %copy-done.7), channel_id=1, source_target_pairs={{0,13},{2,15},{4,9},{6,11},{8,5},{10,7},{12,1},{14,3},{16,29},{18,... | collective-permute-start | bytes 442376 | tf_op jit(solution)/shard_map/ppermute | solution.py:604
  16.1 1.3 %collective-permute-start.1 = (bf16[8,72,128]{2,1,0:T(8,128)(2,1)S(1)}, bf16[8,72,128]{2,1,0:T(8,128)(2,1)S(1)}, u32[]{:S(2)}, u32[]{:S(2)}) collective-permute-start(bf16[8,72,128]{2,1,0:T(8,128)(2,1)S(1)} %copy-done.6), channel_id=1, source_target_pairs={{0,15},{2,13},{4,11},{6,9},{8,7},{10,5},{12,3},{14,1},{16,31},{18,... | collective-permute-start | bytes 442376 | tf_op jit(solution)/shard_map/ppermute | solution.py:604
  17.4 1.3 %collective-permute-start.3 = (bf16[8,72,128]{2,1,0:T(8,128)(2,1)}, bf16[8,72,128]{2,1,0:T(8,128)(2,1)S(1)}, u32[]{:S(2)}, u32[]{:S(2)}) collective-permute-start(bf16[8,72,128]{2,1,0:T(8,128)(2,1)} %get-tuple-element.33), channel_id=1, source_target_pairs={{0,3},{2,1},{4,7},{6,5},{8,11},{10,9},{12,15},{14,13},{16,19},{18,... | collective-permute-start | bytes 442376 | tf_op jit(solution)/shard_map/ppermute | solution.py:604
  18.7 1.3 %collective-permute-start.4 = (bf16[8,72,128]{2,1,0:T(8,128)(2,1)}, bf16[8,72,128]{2,1,0:T(8,128)(2,1)S(1)}, u32[]{:S(2)}, u32[]{:S(2)}) collective-permute-start(bf16[8,72,128]{2,1,0:T(8,128)(2,1)} %get-tuple-element.34), channel_id=1, source_target_pairs={{0,5},{2,7},{4,1},{6,3},{8,13},{10,15},{12,9},{14,11},{16,21},{18,... | collective-permute-start | bytes 442376 | tf_op jit(solution)/shard_map/ppermute | solution.py:604
  20.0 0.0 collective-permute-done.2.rest_0_
  20.0 0.0 copy-done.5
  20.0 1.3 %collective-permute-start.5 = (bf16[8,72,128]{2,1,0:T(8,128)(2,1)S(1)}, bf16[8,72,128]{2,1,0:T(8,128)(2,1)S(1)}, u32[]{:S(2)}, u32[]{:S(2)}) collective-permute-start(bf16[8,72,128]{2,1,0:T(8,128)(2,1)S(1)} %copy-done.5), channel_id=1, source_target_pairs={{0,7},{2,5},{4,3},{6,1},{8,15},{10,13},{12,11},{14,9},{16,23},{18,... | collective-permute-start | bytes 442376 | tf_op jit(solution)/shard_map/ppermute | solution.py:604
  21.3 17.2 %collective-permute-done.rest_0_ = bf16[8,72,128]{2,1,0:T(8,128)(2,1)S(1)} collective-permute-done((bf16[8,72,128]{2,1,0:T(8,128)(2,1)S(1)}, bf16[8,72,128]{2,1,0:T(8,128)(2,1)S(1)}, u32[]{:S(2)}, u32[]{:S(2)}) %collective-permute-start) | collective-permute-done | bytes 147488 | tf_op jit(solution)/shard_map/ppermute | solution.py:604
  38.5 0.0 copy-done.4
  38.5 1.3 %collective-permute-start.6 = (bf16[8,72,128]{2,1,0:T(8,128)(2,1)S(1)}, bf16[8,72,128]{2,1,0:T(8,128)(2,1)S(1)}, u32[]{:S(2)}, u32[]{:S(2)}) collective-permute-start(bf16[8,72,128]{2,1,0:T(8,128)(2,1)S(1)} %copy-done.4), channel_id=1, source_target_pairs={{0,9},{2,11},{4,13},{6,15},{8,1},{10,3},{12,5},{14,7},{16,25},{18,... | collective-permute-start | bytes 442376 | tf_op jit(solution)/shard_map/ppermute | solution.py:604
  39.8 1.2 %collective-permute-done.1.rest_1_ = bf16[8,72,128]{2,1,0:T(8,128)(2,1)S(1)} collective-permute-done((bf16[8,72,128]{2,1,0:T(8,128)(2,1)S(1)}, bf16[8,72,128]{2,1,0:T(8,128)(2,1)S(1)}, u32[]{:S(2)}, u32[]{:S(2)}) %collective-permute-start.1) | collective-permute-done | bytes 147488 | tf_op jit(solution)/shard_map/ppermute | solution.py:604
  41.0 1.3 %collective-permute-start.7 = (bf16[8,72,128]{2,1,0:T(8,128)(2,1)S(1)}, bf16[8,72,128]{2,1,0:T(8,128)(2,1)S(1)}, u32[]{:S(2)}, u32[]{:S(2)}) collective-permute-start(bf16[8,72,128]{2,1,0:T(8,128)(2,1)S(1)} %copy-done.3), channel_id=1, source_target_pairs={{0,11},{2,9},{4,15},{6,13},{8,3},{10,1},{12,7},{14,5},{16,27},{18,... | collective-permute-start | bytes 442376 | tf_op jit(solution)/shard_map/ppermute | solution.py:604
  42.3 0.1 copy.17
  42.4 0.2 reshape.36.taps_ref.first_taps_ref
  42.6 0.1 copy.16
  42.7 0.2 reshape.38.second_taps_ref
  42.9 0.0 copy-done.9
  42.9 0.1 broadcast_in_dim.12.gain_ref
  43.0 0.0 collective-permute-done.3.rest_1_
  43.0 0.0 collective-permute-done.4.rest_2_
  43.0 0.0 collective-permute-done.5.rest_3_
  43.0 8.0 %collective-permute-done.6.rest_4_ = bf16[8,72,128]{2,1,0:T(8,128)(2,1)S(1)} collective-permute-done((bf16[8,72,128]{2,1,0:T(8,128)(2,1)S(1)}, bf16[8,72,128]{2,1,0:T(8,128)(2,1)S(1)}, u32[]{:S(2)}, u32[]{:S(2)}) %collective-permute-start.6) | collective-permute-done | bytes 147488 | tf_op jit(solution)/shard_map/ppermute | solution.py:604
  51.0 2.5 %collective-permute-done.7.rest_5_ = bf16[8,72,128]{2,1,0:T(8,128)(2,1)S(1)} collective-permute-done((bf16[8,72,128]{2,1,0:T(8,128)(2,1)S(1)}, bf16[8,72,128]{2,1,0:T(8,128)(2,1)S(1)}, u32[]{:S(2)}, u32[]{:S(2)}) %collective-permute-start.7) | collective-permute-done | bytes 147488 | tf_op jit(solution)/shard_map/ppermute | solution.py:604
  53.5 0.0 all-to-all-done.same
  53.5 1.9 %early_rows.1.before = f32[33,72,128]{2,1,0:T(8,128)S(1)} custom-call(bf16[64,72,128]{2,1,0:T(8,128)(2,1)S(1)} %all-to-all-done.same, bf16[8,72,128]{2,1,0:T(8,128)(2,1)S(1)} %collective-permute-done.2.rest_0_, bf16[8,72,128]{2,1,0:T(8,128)(2,1)S(1)} %collective-permute-done.3.rest_1_, bf16[8,72,128]{2,1,0:T(8,128)(2,1)S(1)} %collective-permute-done.4.rest_2_, ...), custom_call_target="tpu_custom_call" | custom-call | flops 2097152 | bytes 4194304 | tf_op jit(solution)/shard_map/early_rows/pallas_call | solution.py:213
  55.5 2.1 %gather_rows.1 = (bf16[32,72,128]{2,1,0:T(8,128)(2,1)S(1)}, bf16[32,80,128]{2,1,0:T(8,128)(2,1)S(1)}, bf16[3,80,128]{2,1,0:T(8,128)(2,1)S(1)}, bf16[3,80,128]{2,1,0:T(8,128)(2,1)S(1)}, bf16[80,128]{1,0:T(8,128)(2,1)S(1)}) custom-call(s32[1,2]{1,0:T(1,128)S(1)} %copy-done, f32[72,128]{1,0:T(8,128)S(1)} %broadcast_in_dim.12.gain_ref, ...), custom_call_target="tpu_custom_call" | custom-call | tf_op jit(solution)/shard_map/gather_rows/pallas_call | solution.py:285
  57.6 0.9 %collective-permute-start.8 = (bf16[3,80,128]{2,1,0:T(8,128)(2,1)S(1)}, bf16[3,80,128]{2,1,0:T(8,128)(2,1)S(1)}, u32[]{:S(2)}, u32[]{:S(2)}) collective-permute-start(bf16[3,80,128]{2,1,0:T(8,128)(2,1)S(1)} %get-tuple-element.44), channel_id=1, source_target_pairs={{0,1},{1,2},{2,3},{3,4},{4,5},{5,6},{6,7},{7,8},{8,9},{9,10},{10,1... | collective-permute-start | bytes 184328 | tf_op jit(solution)/shard_map/ppermute | solution.py:587
  58.5 0.0 collective-permute-start.9
  58.5 1.2 %inner_convolution.1 = (bf16[32,80,128]{2,1,0:T(8,128)(2,1)S(1)}, f32[2,80,128]{2,1,0:T(8,128)S(1)}, f32[2,80,128]{2,1,0:T(8,128)S(1)}) custom-call(bf16[240,240]{1,0:T(8,128)(2,1)S(1)} %reshape.36.taps_ref.first_taps_ref, bf16[32,80,128]{2,1,0:T(8,128)(2,1)S(1)} %get-tuple-element.43.field), custom_call_target="tpu_custom_call" | custom-call | flops 471859200 | bytes 2097152 | tf_op jit(solution)/shard_map/inner_convolution/pallas_call | solution.py:369
  59.7 0.1 collective-permute-done.8.above
  59.8 2.6 %collective-permute-done.9.below = bf16[3,80,128]{2,1,0:T(8,128)(2,1)S(1)} collective-permute-done((bf16[3,80,128]{2,1,0:T(8,128)(2,1)S(1)}, bf16[3,80,128]{2,1,0:T(8,128)(2,1)S(1)}, u32[]{:S(2)}, u32[]{:S(2)}) %collective-permute-start.9) | collective-permute-done | bytes 61472 | tf_op jit(solution)/shard_map/ppermute | solution.py:587
  62.4 2.1 %collective-permute-start.10 = (bf16[3,80,128]{2,1,0:T(8,128)(2,1)S(1)}, bf16[3,80,128]{2,1,0:T(8,128)(2,1)S(1)}, u32[]{:S(2)}, u32[]{:S(2)}) collective-permute-start(bf16[3,80,128]{2,1,0:T(8,128)(2,1)S(1)} %pad_maximum_fusion), channel_id=1, source_target_pairs={{0,3},{1,4},{2,5},{3,6},{4,7},{5,8},{6,9},{7,10},{8,11},{9,12},{10... | collective-permute-start | bytes 184328 | tf_op jit(solution)/shard_map/ppermute | solution.py:587
  64.6 2.4 %collective-permute-start.11 = (bf16[3,80,128]{2,1,0:T(8,128)(2,1)S(1)}, bf16[3,80,128]{2,1,0:T(8,128)(2,1)S(1)}, u32[]{:S(2)}, u32[]{:S(2)}) collective-permute-start(bf16[3,80,128]{2,1,0:T(8,128)(2,1)S(1)} %pad_maximum_fusion), channel_id=1, source_target_pairs={{0,13},{1,14},{2,15},{3,0},{4,1},{5,2},{6,3},{7,4},{8,5},{9,6},{10... | collective-permute-start | bytes 184328 | tf_op jit(solution)/shard_map/ppermute | solution.py:587
  66.9 2.0 %channels_first.1 = bf16[2208,128]{1,0:T(8,128)(2,1)} custom-call(bf16[32,72,128]{2,1,0:T(8,128)(2,1)S(1)} %get-tuple-element.40.field.gridded), custom_call_target="tpu_custom_call" | custom-call | tf_op jit(solution)/shard_map/channels_first/pallas_call | solution.py:303
  68.9 0.1 collective-permute-done.10.rest_0_
  69.0 0.6 collective-permute-done.11.rest_1_
  69.6 3.7 %convolutions.1 = bf16[2208,128]{1,0:T(8,128)(2,1)} custom-call(bf16[240,240]{1,0:T(8,128)(2,1)S(1)} %reshape.36.taps_ref.first_taps_ref, bf16[240,240]{1,0:T(8,128)(2,1)S(1)} %reshape.38.second_taps_ref, bf16[32,80,128]{2,1,0:T(8,128)(2,1)S(1)} %get-tuple-element.43.field, bf16[32,72,128]{2,1,0:T(8,128)(2,1)S(1)} %get-tuple-element.40.field.gridded, ...), custom_call_target="tpu_custom_call" | custom-call | tf_op jit(solution)/shard_map/convolutions/pallas_call | solution.py:564
  (15 shorter events, 0.1 us)
Async XLA Ops:
  6.8 6.6 %copy-start.8 = (bf16[8,72,128]{2,1,0:T(8,128)(2,1)S(1)}, bf16[8,72,128]{2,1,0:T(8,128)(2,1)}, u32[]{:S(2)}) copy-start(bf16[8,72,128]{2,1,0:T(8,128)(2,1)} %get-tuple-element.32) | copy-start | bytes 442372
  6.9 7.9 %copy-start.7 = (bf16[8,72,128]{2,1,0:T(8,128)(2,1)S(1)}, bf16[8,72,128]{2,1,0:T(8,128)(2,1)}, u32[]{:S(2)}) copy-start(bf16[8,72,128]{2,1,0:T(8,128)(2,1)} %get-tuple-element.28) | copy-start | bytes 442372
  6.9 9.2 %copy-start.6 = (bf16[8,72,128]{2,1,0:T(8,128)(2,1)S(1)}, bf16[8,72,128]{2,1,0:T(8,128)(2,1)}, u32[]{:S(2)}) copy-start(bf16[8,72,128]{2,1,0:T(8,128)(2,1)} %get-tuple-element.29) | copy-start | bytes 442372
  6.9 13.1 %copy-start.5 = (bf16[8,72,128]{2,1,0:T(8,128)(2,1)S(1)}, bf16[8,72,128]{2,1,0:T(8,128)(2,1)}, u32[]{:S(2)}) copy-start(bf16[8,72,128]{2,1,0:T(8,128)(2,1)} %get-tuple-element.35) | copy-start | bytes 442372
  6.9 31.6 %copy-start.4 = (bf16[8,72,128]{2,1,0:T(8,128)(2,1)S(1)}, bf16[8,72,128]{2,1,0:T(8,128)(2,1)}, u32[]{:S(2)}) copy-start(bf16[8,72,128]{2,1,0:T(8,128)(2,1)} %get-tuple-element.36) | copy-start | bytes 442372
  6.9 34.1 %copy-start.3 = (bf16[8,72,128]{2,1,0:T(8,128)(2,1)S(1)}, bf16[8,72,128]{2,1,0:T(8,128)(2,1)}, u32[]{:S(2)}) copy-start(bf16[8,72,128]{2,1,0:T(8,128)(2,1)} %get-tuple-element.37) | copy-start | bytes 442372
  6.9 35.3 %copy-start.1 = (bf16[9,69,69]{2,1,0:T(8,128)(2,1)S(1)}, bf16[9,69,69]{2,1,0:T(8,128)(2,1)}, u32[]{:S(2)}) copy-start(bf16[9,69,69]{2,1,0:T(8,128)(2,1)} %param.14) | copy-start | bytes 257098
  6.9 35.6 %copy-start.2 = (bf16[9,69,69]{2,1,0:T(8,128)(2,1)S(1)}, bf16[9,69,69]{2,1,0:T(8,128)(2,1)}, u32[]{:S(2)}) copy-start(bf16[9,69,69]{2,1,0:T(8,128)(2,1)} %param.15) | copy-start | bytes 257098
  6.9 46.6 %all-to-all-start = ((bf16[64,72,128]{2,1,0:T(8,128)(2,1)}), bf16[64,72,128]{2,1,0:T(8,128)(2,1)S(1)}, u32[]{:S(2)}, u32[]{:S(2)}) async-start(bf16[64,72,128]{2,1,0:T(8,128)(2,1)} %get-tuple-element.31), calls=%async_computation | async-start | bytes 2359296 | tf_op jit(solution)/shard_map/all_to_all | solution.py:605
  13.5 29.4 %copy-start.9 = (f32[69]{0:T(128)S(1)}, f32[69]{0:T(128)}, u32[]{:S(2)}) copy-start(f32[69]{0:T(128)} %param.13) | copy-start | bytes 832
  13.5 6.5 %collective-permute-start.2 = (bf16[8,72,128]{2,1,0:T(8,128)(2,1)S(1)}, bf16[8,72,128]{2,1,0:T(8,128)(2,1)S(1)}, u32[]{:S(2)}, u32[]{:S(2)}) collective-permute-start(bf16[8,72,128]{2,1,0:T(8,128)(2,1)S(1)} %copy-done.8), channel_id=1, source_target_pairs={{0,1},{2,3},{4,5},{6,7},{8,9},{10,11},{12,13},{14,15},{16,17},{18,... | collective-permute-start | bytes 442376 | tf_op jit(solution)/shard_map/ppermute | solution.py:604
  14.8 23.7 %collective-permute-start = (bf16[8,72,128]{2,1,0:T(8,128)(2,1)S(1)}, bf16[8,72,128]{2,1,0:T(8,128)(2,1)S(1)}, u32[]{:S(2)}, u32[]{:S(2)}) collective-permute-start(bf16[8,72,128]{2,1,0:T(8,128)(2,1)S(1)} %copy-done.7), channel_id=1, source_target_pairs={{0,13},{2,15},{4,9},{6,11},{8,5},{10,7},{12,1},{14,3},{16,29},{18,... | collective-permute-start | bytes 442376 | tf_op jit(solution)/shard_map/ppermute | solution.py:604
  16.1 24.9 %collective-permute-start.1 = (bf16[8,72,128]{2,1,0:T(8,128)(2,1)S(1)}, bf16[8,72,128]{2,1,0:T(8,128)(2,1)S(1)}, u32[]{:S(2)}, u32[]{:S(2)}) collective-permute-start(bf16[8,72,128]{2,1,0:T(8,128)(2,1)S(1)} %copy-done.6), channel_id=1, source_target_pairs={{0,15},{2,13},{4,11},{6,9},{8,7},{10,5},{12,3},{14,1},{16,31},{18,... | collective-permute-start | bytes 442376 | tf_op jit(solution)/shard_map/ppermute | solution.py:604
  17.4 25.6 %collective-permute-start.3 = (bf16[8,72,128]{2,1,0:T(8,128)(2,1)}, bf16[8,72,128]{2,1,0:T(8,128)(2,1)S(1)}, u32[]{:S(2)}, u32[]{:S(2)}) collective-permute-start(bf16[8,72,128]{2,1,0:T(8,128)(2,1)} %get-tuple-element.33), channel_id=1, source_target_pairs={{0,3},{2,1},{4,7},{6,5},{8,11},{10,9},{12,15},{14,13},{16,19},{18,... | collective-permute-start | bytes 442376 | tf_op jit(solution)/shard_map/ppermute | solution.py:604
  18.7 24.3 %collective-permute-start.4 = (bf16[8,72,128]{2,1,0:T(8,128)(2,1)}, bf16[8,72,128]{2,1,0:T(8,128)(2,1)S(1)}, u32[]{:S(2)}, u32[]{:S(2)}) collective-permute-start(bf16[8,72,128]{2,1,0:T(8,128)(2,1)} %get-tuple-element.34), channel_id=1, source_target_pairs={{0,5},{2,7},{4,1},{6,3},{8,13},{10,15},{12,9},{14,11},{16,21},{18,... | collective-permute-start | bytes 442376 | tf_op jit(solution)/shard_map/ppermute | solution.py:604
  20.0 23.0 %collective-permute-start.5 = (bf16[8,72,128]{2,1,0:T(8,128)(2,1)S(1)}, bf16[8,72,128]{2,1,0:T(8,128)(2,1)S(1)}, u32[]{:S(2)}, u32[]{:S(2)}) collective-permute-start(bf16[8,72,128]{2,1,0:T(8,128)(2,1)S(1)} %copy-done.5), channel_id=1, source_target_pairs={{0,7},{2,5},{4,3},{6,1},{8,15},{10,13},{12,11},{14,9},{16,23},{18,... | collective-permute-start | bytes 442376 | tf_op jit(solution)/shard_map/ppermute | solution.py:604
  38.5 12.5 %collective-permute-start.6 = (bf16[8,72,128]{2,1,0:T(8,128)(2,1)S(1)}, bf16[8,72,128]{2,1,0:T(8,128)(2,1)S(1)}, u32[]{:S(2)}, u32[]{:S(2)}) collective-permute-start(bf16[8,72,128]{2,1,0:T(8,128)(2,1)S(1)} %copy-done.4), channel_id=1, source_target_pairs={{0,9},{2,11},{4,13},{6,15},{8,1},{10,3},{12,5},{14,7},{16,25},{18,... | collective-permute-start | bytes 442376 | tf_op jit(solution)/shard_map/ppermute | solution.py:604
  41.0 12.6 %collective-permute-start.7 = (bf16[8,72,128]{2,1,0:T(8,128)(2,1)S(1)}, bf16[8,72,128]{2,1,0:T(8,128)(2,1)S(1)}, u32[]{:S(2)}, u32[]{:S(2)}) collective-permute-start(bf16[8,72,128]{2,1,0:T(8,128)(2,1)S(1)} %copy-done.3), channel_id=1, source_target_pairs={{0,11},{2,9},{4,15},{6,13},{8,3},{10,1},{12,7},{14,5},{16,27},{18,... | collective-permute-start | bytes 442376 | tf_op jit(solution)/shard_map/ppermute | solution.py:604
  43.0 12.5 %copy-start = (s32[1,2]{1,0:T(1,128)S(1)}, s32[1,2]{1,0:T(1,128)}, u32[]{:S(2)}) copy-start(s32[1,2]{1,0:T(1,128)} %flip_ref.1) | copy-start | bytes 28
  57.6 2.2 %collective-permute-start.8 = (bf16[3,80,128]{2,1,0:T(8,128)(2,1)S(1)}, bf16[3,80,128]{2,1,0:T(8,128)(2,1)S(1)}, u32[]{:S(2)}, u32[]{:S(2)}) collective-permute-start(bf16[3,80,128]{2,1,0:T(8,128)(2,1)S(1)} %get-tuple-element.44), channel_id=1, source_target_pairs={{0,1},{1,2},{2,3},{3,4},{4,5},{5,6},{6,7},{7,8},{8,9},{9,10},{10,1... | collective-permute-start | bytes 184328 | tf_op jit(solution)/shard_map/ppermute | solution.py:587
  58.5 3.9 %collective-permute-start.9 = (bf16[3,80,128]{2,1,0:T(8,128)(2,1)S(1)}, bf16[3,80,128]{2,1,0:T(8,128)(2,1)S(1)}, u32[]{:S(2)}, u32[]{:S(2)}) collective-permute-start(bf16[3,80,128]{2,1,0:T(8,128)(2,1)S(1)} %get-tuple-element.46), channel_id=1, source_target_pairs={{0,15},{1,0},{2,1},{3,2},{4,3},{5,4},{6,5},{7,6},{8,7},{9,8},{10,9... | collective-permute-start | bytes 184328 | tf_op jit(solution)/shard_map/ppermute | solution.py:587
  62.4 6.5 %collective-permute-start.10 = (bf16[3,80,128]{2,1,0:T(8,128)(2,1)S(1)}, bf16[3,80,128]{2,1,0:T(8,128)(2,1)S(1)}, u32[]{:S(2)}, u32[]{:S(2)}) collective-permute-start(bf16[3,80,128]{2,1,0:T(8,128)(2,1)S(1)} %pad_maximum_fusion), channel_id=1, source_target_pairs={{0,3},{1,4},{2,5},{3,6},{4,7},{5,8},{6,9},{7,10},{8,11},{9,12},{10... | collective-permute-start | bytes 184328 | tf_op jit(solution)/shard_map/ppermute | solution.py:587
  64.6 5.1 %collective-permute-start.11 = (bf16[3,80,128]{2,1,0:T(8,128)(2,1)S(1)}, bf16[3,80,128]{2,1,0:T(8,128)(2,1)S(1)}, u32[]{:S(2)}, u32[]{:S(2)}) collective-permute-start(bf16[3,80,128]{2,1,0:T(8,128)(2,1)S(1)} %pad_maximum_fusion), channel_id=1, source_target_pairs={{0,13},{1,14},{2,15},{3,0},{4,1},{5,2},{6,3},{7,4},{8,5},{9,6},{10... | collective-permute-start | bytes 184328 | tf_op jit(solution)/shard_map/ppermute | solution.py:587
